TPU v7x, 32 devices: a whole 2x2x4 slice. The times are simulated.
32 devices in a mesh: dp: 4 (over y, x), fsdp: 8 (over z, core).
Axes of the slice: x: 2, y: 2, z: 4, core: 2. Of those that a mesh axis runs over, the one named last changes fastest.
Arguments:
- hidden: bfloat16 [50176, 768], P(('dp', 'fsdp')), may hold values from -6 to 6
- cotangent: bfloat16 [50176, 768], P(('dp', 'fsdp')), may hold values from -6 to 6
- drive_weight: bfloat16 [4608, 128], P(('dp', 'fsdp')), may hold values from -0.21875 to 0.21875
- forget_weight: bfloat16 [2304, 128], P(('dp', 'fsdp')), may hold values from -0.21875 to 0.21875
- outgate_weight: bfloat16 [4608, 128], P(('dp', 'fsdp')), may hold values from -0.21875 to 0.21875
- mixout_weight: bfloat16 [4608, 128], P(('dp', 'fsdp')), may hold values from -0.4375 to 0.4375
- gate_weight: bfloat16 [9216, 128], P(('dp', 'fsdp')), may hold values from -0.21875 to 0.21875
- up_weight: bfloat16 [9216, 128], P(('dp', 'fsdp')), may hold values from -0.21875 to 0.21875
- down_weight: bfloat16 [9216, 128], P(('dp', 'fsdp')), may hold values from -0.21875 to 0.21875
- first_gain: bfloat16 [768], P(('dp', 'fsdp')), may hold values from 0.099609375 to 1.8984375
- second_gain: bfloat16 [768], P(('dp', 'fsdp')), may hold values from 0.099609375 to 1.8984375
- group_gain: bfloat16 [768], P(('dp', 'fsdp')), may hold values from 0.099609375 to 1.8984375
- forget_bias: bfloat16 [384], P(('dp', 'fsdp')), may hold values from -1 to 6
- phase_angle: bfloat16 [384], P(('dp', 'fsdp')), may hold values from -3.140625 to 3.140625
Outputs:
- layer_out: bfloat16 [50176, 768], P(('dp', 'fsdp'))
- hidden_grad: float32 [50176, 768], P(('dp', 'fsdp'))
- drive_grad: float32 [4608, 128], P(('dp', 'fsdp'))
- forget_grad: float32 [2304, 128], P(('dp', 'fsdp'))
- outgate_grad: float32 [4608, 128], P(('dp', 'fsdp'))
- mixout_grad: float32 [4608, 128], P(('dp', 'fsdp'))
- gate_grad: float32 [9216, 128], P(('dp', 'fsdp'))
- up_grad: float32 [9216, 128], P(('dp', 'fsdp'))
- down_grad: float32 [9216, 128], P(('dp', 'fsdp'))
- firstgain_grad: float32 [768], P(('dp', 'fsdp'))
- secondgain_grad: float32 [768], P(('dp', 'fsdp'))
- groupgain_grad: float32 [768], P(('dp', 'fsdp'))
- bias_grad: float32 [384], P(('dp', 'fsdp'))
- phase_grad: float32 [384], P(('dp', 'fsdp'))
All inputs are finite; a program needn't handle non-finite values.
Results may differ from a plain program's by a relative error of at most 0.013.
Values may be sent and summed in bfloat16 or wider, within the bound.
A program may use at most 256 MiB of HBM per device.

v0:
```python
import jax
import jax.numpy as jnp
from jax import lax
from jax.sharding import PartitionSpec as P

D = 768
C = 384
FF = 1536
SPAN = 56
GROUPS = 8


lower_bound = 0.25
norm_eps = 1e-06
group_eps = 1e-05


def product(left, right):
    return jnp.dot(left, right, preferred_element_type=jnp.float32)


def outer_sum(left, right):
    return lax.dot_general(
        left, right, (((0,), (0,)), ((), ())), preferred_element_type=jnp.float32
    )


def back_product(left, right):
    return lax.dot_general(
        left, right, (((1,), (1,)), ((), ())), preferred_element_type=jnp.float32
    )


def rms_scale(values, gain_vec):
    return (
        values * lax.rsqrt(jnp.mean(values * values, axis=1, keepdims=True) + norm_eps) * gain_vec
    )


def combine(earlier, later_term):
    return (
        later_term[0] * earlier[0] - later_term[1] * earlier[1],
        later_term[0] * earlier[1] + later_term[1] * earlier[0],
        later_term[0] * earlier[2] - later_term[1] * earlier[3] + later_term[2],
        later_term[0] * earlier[3] + later_term[1] * earlier[2] + later_term[3],
    )


def block_prefix(block_terms):
    length = block_terms[0].shape[0]
    width = block_terms[0].shape[1]
    current = block_terms
    offset = 1
    while offset < length:
        filler = (
            jnp.ones((offset, width), jnp.float32),
            jnp.zeros((offset, width), jnp.float32),
            jnp.zeros((offset, width), jnp.float32),
            jnp.zeros((offset, width), jnp.float32),
        )
        earlier = tuple(
            (
                jnp.concatenate([front, member[: length - offset]], axis=0)
                for front, member in zip(filler, current)
            )
        )
        current = combine(earlier, current)
        offset = offset * 2
    return current


def mixer_core(drive_pre, forget_pre, outgate_pre, phase_angle, forget_bias, group_gain):
    length = drive_pre.shape[0]
    features = drive_pre.shape[1]
    channels = features // 2
    blocks = length // SPAN
    driven = jax.nn.silu(drive_pre)
    retain = lower_bound + (1.0 - lower_bound) * jax.nn.sigmoid(forget_pre + forget_bias)
    rotate_re = retain * jnp.cos(phase_angle)
    rotate_im = retain * jnp.sin(phase_angle)
    inflow = 1.0 - retain
    source_re = inflow * driven[:, :channels]
    source_im = inflow * driven[:, channels:]
    pieces = tuple(
        (
            member.reshape(blocks, SPAN, channels)
            for member in (rotate_re, rotate_im, source_re, source_im)
        )
    )

    def advance(carried, block_terms):
        summed = block_prefix(block_terms)
        state_re = summed[0] * carried[0] - summed[1] * carried[1] + summed[2]
        state_im = summed[0] * carried[1] + summed[1] * carried[0] + summed[3]
        return ((state_re[-1], state_im[-1]), (state_re, state_im))

    initial = (jnp.zeros((channels,), jnp.float32), jnp.zeros((channels,), jnp.float32))
    _, (states_re, states_im) = lax.scan(jax.checkpoint(advance), initial, pieces)
    joined = jnp.concatenate(
        [states_re.reshape(length, channels), states_im.reshape(length, channels)], axis=1
    )
    grouped = joined.reshape(length, GROUPS, features // GROUPS)
    centered = grouped - jnp.mean(grouped, axis=2, keepdims=True)
    normed = centered * lax.rsqrt(jnp.mean(centered * centered, axis=2, keepdims=True) + group_eps)
    return normed.reshape(length, features) * group_gain * jax.nn.sigmoid(outgate_pre)


def unpack(gathered):
    targets = ((D, D), (D, C), (D, D), (D, D), (D, FF), (D, FF), (FF, D))
    matrices = tuple(
        (gathered[position].reshape(target) for position, target in enumerate(targets))
    )
    vectors = tuple((member.astype(jnp.float32) for member in gathered[7:]))
    return matrices + vectors


def local(
    hidden,
    cotangent,
    drive_weight,
    forget_weight,
    outgate_weight,
    mixout_weight,
    gate_weight,
    up_weight,
    down_weight,
    first_gain,
    second_gain,
    group_gain,
    forget_bias,
    phase_angle,
):
    params = unpack(
        (
            lax.all_gather(drive_weight, ("dp", "fsdp"), axis=0, tiled=True),
            lax.all_gather(forget_weight, ("dp", "fsdp"), axis=0, tiled=True),
            lax.all_gather(outgate_weight, ("dp", "fsdp"), axis=0, tiled=True),
            lax.all_gather(mixout_weight, ("dp", "fsdp"), axis=0, tiled=True),
            lax.all_gather(gate_weight, ("dp", "fsdp"), axis=0, tiled=True),
            lax.all_gather(up_weight, ("dp", "fsdp"), axis=0, tiled=True),
            lax.all_gather(down_weight, ("dp", "fsdp"), axis=0, tiled=True),
            lax.all_gather(first_gain, ("dp", "fsdp"), axis=0, tiled=True),
            lax.all_gather(second_gain, ("dp", "fsdp"), axis=0, tiled=True),
            lax.all_gather(group_gain, ("dp", "fsdp"), axis=0, tiled=True),
            lax.all_gather(forget_bias, ("dp", "fsdp"), axis=0, tiled=True),
            lax.all_gather(phase_angle, ("dp", "fsdp"), axis=0, tiled=True),
        )
    )
    inputs = hidden.astype(jnp.float32)
    normed_float, pull_first = jax.vjp(rms_scale, inputs, params[7])
    normed_one = normed_float.astype(jnp.bfloat16)
    drive_pre = product(normed_one, params[0])
    forget_pre = product(normed_one, params[1])
    outgate_pre = product(normed_one, params[2])
    mixed_float, pull_mixer = jax.vjp(
        mixer_core, drive_pre, forget_pre, outgate_pre, params[11], params[10], params[9]
    )
    mixed = mixed_float.astype(jnp.bfloat16)
    middle = inputs + product(mixed, params[3])
    second_float, pull_second = jax.vjp(rms_scale, middle, params[8])
    normed_two = second_float.astype(jnp.bfloat16)
    gate_pre = product(normed_two, params[4])
    up_pre = product(normed_two, params[5])
    gate_sig = jax.nn.sigmoid(gate_pre)
    silu_gate = gate_pre * gate_sig
    hidden_units = (silu_gate * up_pre).astype(jnp.bfloat16)
    layer_out = (middle + product(hidden_units, params[6])).astype(jnp.bfloat16)
    back_params = unpack(
        (
            lax.all_gather(drive_weight, ("dp", "fsdp"), axis=0, tiled=True),
            lax.all_gather(forget_weight, ("dp", "fsdp"), axis=0, tiled=True),
            lax.all_gather(outgate_weight, ("dp", "fsdp"), axis=0, tiled=True),
            lax.all_gather(mixout_weight, ("dp", "fsdp"), axis=0, tiled=True),
            lax.all_gather(gate_weight, ("dp", "fsdp"), axis=0, tiled=True),
            lax.all_gather(up_weight, ("dp", "fsdp"), axis=0, tiled=True),
            lax.all_gather(down_weight, ("dp", "fsdp"), axis=0, tiled=True),
            lax.all_gather(first_gain, ("dp", "fsdp"), axis=0, tiled=True),
            lax.all_gather(second_gain, ("dp", "fsdp"), axis=0, tiled=True),
            lax.all_gather(group_gain, ("dp", "fsdp"), axis=0, tiled=True),
            lax.all_gather(forget_bias, ("dp", "fsdp"), axis=0, tiled=True),
            lax.all_gather(phase_angle, ("dp", "fsdp"), axis=0, tiled=True),
        )
    )
    units_back = back_product(cotangent, back_params[6])
    down_grad = outer_sum(hidden_units, cotangent)
    slope = gate_sig * (1.0 + gate_pre * (1.0 - gate_sig))
    gate_back = (units_back * up_pre * slope).astype(jnp.bfloat16)
    up_back = (units_back * silu_gate).astype(jnp.bfloat16)
    gate_grad = outer_sum(normed_two, gate_back)
    up_grad = outer_sum(normed_two, up_back)
    second_back = back_product(gate_back, back_params[4]) + back_product(up_back, back_params[5])
    middle_part, secondgain_grad = pull_second(second_back)
    middle_back = cotangent.astype(jnp.float32) + middle_part
    middle_low = middle_back.astype(jnp.bfloat16)
    mixout_grad = outer_sum(mixed, middle_low)
    mixed_back = back_product(middle_low, back_params[3])
    drive_back, forget_back, outgate_back, phase_grad, bias_grad, groupgain_grad = pull_mixer(
        mixed_back
    )
    drive_low = drive_back.astype(jnp.bfloat16)
    forget_low = forget_back.astype(jnp.bfloat16)
    outgate_low = outgate_back.astype(jnp.bfloat16)
    drive_grad = outer_sum(normed_one, drive_low)
    forget_grad = outer_sum(normed_one, forget_low)
    outgate_grad = outer_sum(normed_one, outgate_low)
    first_back = (
        back_product(drive_low, back_params[0])
        + back_product(forget_low, back_params[1])
        + back_product(outgate_low, back_params[2])
    )
    input_part, firstgain_grad = pull_first(first_back)
    hidden_grad = middle_back + input_part
    all_terms = (
        drive_grad.reshape(-1, 128),
        forget_grad.reshape(-1, 128),
        outgate_grad.reshape(-1, 128),
        mixout_grad.reshape(-1, 128),
        gate_grad.reshape(-1, 128),
        up_grad.reshape(-1, 128),
        down_grad.reshape(-1, 128),
        firstgain_grad,
        secondgain_grad,
        groupgain_grad,
        bias_grad,
        phase_grad,
    )
    sums = (
        lax.psum_scatter(all_terms[0], ("dp", "fsdp"), scatter_dimension=0, tiled=True),
        lax.psum_scatter(all_terms[1], ("dp", "fsdp"), scatter_dimension=0, tiled=True),
        lax.psum_scatter(all_terms[2], ("dp", "fsdp"), scatter_dimension=0, tiled=True),
        lax.psum_scatter(all_terms[3], ("dp", "fsdp"), scatter_dimension=0, tiled=True),
        lax.psum_scatter(all_terms[4], ("dp", "fsdp"), scatter_dimension=0, tiled=True),
        lax.psum_scatter(all_terms[5], ("dp", "fsdp"), scatter_dimension=0, tiled=True),
        lax.psum_scatter(all_terms[6], ("dp", "fsdp"), scatter_dimension=0, tiled=True),
        lax.psum_scatter(all_terms[7], ("dp", "fsdp"), scatter_dimension=0, tiled=True),
        lax.psum_scatter(all_terms[8], ("dp", "fsdp"), scatter_dimension=0, tiled=True),
        lax.psum_scatter(all_terms[9], ("dp", "fsdp"), scatter_dimension=0, tiled=True),
        lax.psum_scatter(all_terms[10], ("dp", "fsdp"), scatter_dimension=0, tiled=True),
        lax.psum_scatter(all_terms[11], ("dp", "fsdp"), scatter_dimension=0, tiled=True),
    )
    return (
        layer_out,
        hidden_grad,
        sums[0],
        sums[1],
        sums[2],
        sums[3],
        sums[4],
        sums[5],
        sums[6],
        sums[7],
        sums[8],
        sums[9],
        sums[10],
        sums[11],
    )


def solution(mesh):
    in_specs = (
        P(("dp", "fsdp"), None),
        P(("dp", "fsdp"), None),
        P(("dp", "fsdp"), None),
        P(("dp", "fsdp"), None),
        P(("dp", "fsdp"), None),
        P(("dp", "fsdp"), None),
        P(("dp", "fsdp"), None),
        P(("dp", "fsdp"), None),
        P(("dp", "fsdp"), None),
        P(("dp", "fsdp")),
        P(("dp", "fsdp")),
        P(("dp", "fsdp")),
        P(("dp", "fsdp")),
        P(("dp", "fsdp")),
    )
    out_specs = (
        P(("dp", "fsdp"), None),
        P(("dp", "fsdp"), None),
        P(("dp", "fsdp"), None),
        P(("dp", "fsdp"), None),
        P(("dp", "fsdp"), None),
        P(("dp", "fsdp"), None),
        P(("dp", "fsdp"), None),
        P(("dp", "fsdp"), None),
        P(("dp", "fsdp"), None),
        P(("dp", "fsdp")),
        P(("dp", "fsdp")),
        P(("dp", "fsdp")),
        P(("dp", "fsdp")),
        P(("dp", "fsdp")),
    )
    return jax.shard_map(local, mesh=mesh, in_specs=in_specs, out_specs=out_specs, check_vma=False)
```

profile of v0, /device:TPU:0, one launch (start us, length us, event | category | flops | bytes accessed | tf_op | source)
XLA Modules:
  0.0 1447.1 jit_solution(15258996193182667919)
XLA Ops:
  15.5 42.1 %all-reduce.88 = (bf16[768]{0:T(1024)(128)(2,1)S(1)}, bf16[384]{0:T(512)(128)(2,1)S(1)}, bf16[384]{0:T(512)(128)(2,1)S(1)}, bf16[768]{0:T(1024)(128)(2,1)S(1)}, bf16[768]{0:T(1024)(128)(2,1)S(1)}) all-reduce(bf16[768]{0:T(1024)(128)(2,1)S(1)} %dynamic-update-slice, ...), channel_id=1, replica_groups=mesh['dp'=4,'fsdp'=8] {'dp','fsdp'}, use_global_device_ids=true, to_apply=%add.76 | all-reduce | flops 3072 | bytes 12288
  60.4 45.6 %all_gather.44 = bf16[2304,128]{1,0:T(8,128)(2,1)} all-gather(bf16[72,128]{1,0:T(8,128)(2,1)S(1)} %copy-done.29), channel_id=1, replica_groups=mesh['dp'=4,'fsdp'=8] {'dp','fsdp'}, dimensions={0}, use_global_device_ids=true | all-gather | bytes 608256 | tf_op jit(solution)/shard_map/all_gather | solution.py:136
  124.6 151.0 %while.45 = (s32[]{:T(128)}, f32[384]{0:T(512)S(1)}, f32[384]{0:T(512)S(1)}, f32[28,56,384]{2,1,0:T(8,128)S(1)}, f32[28,56,384]{2,1,0:T(8,128)}, /*index=5*/f32[...) while((s32[]{:T(128)}, f32[384]{0:T(512)S(1)}, ...), condition=%wide.region_2.3_spmd, body=%wide.region_1.2_spmd.sunk | while | flops 1978370 | bytes 9165461 | solution.py:98
  293.6 25.4 %multiply_reduce_fusion.5 = (f32[1568,8]{1,0:T(8,128)}, f32[1568,8,96]{2,1,0:T(8,128)}) fusion(f32[1568,8]{1,0:T(8,128)} %copy.70, f32[1568,4,96]{2,1,0:T(4,128)} %concatenate.153, f32[1568,4,96]{2,1,0:T(4,128)S(1)} %concatenate.152), kind=kLoop, calls=%fused_computation.268 | loop fusion | flops 4804352 | bytes 9734144 | tf_op jit(solution)/shard_map/jvp()/reduce_sum | solution.py:104
  323.3 6.1 copy.76
  329.4 6.9 copy.71
  349.2 8.1 multiply_convert_fusion.4
  374.0 8.1 fusion.158
  382.1 6.2 fusion.159
  393.7 16.8 %multiply_convert_fusion = (bf16[1568,1536]{1,0:T(8,128)(2,1)}, bf16[1568,1536]{1,0:T(8,128)(2,1)}, bf16[1568,1536]{1,0:T(8,128)(2,1)}) fusion(f32[1568,1536]{1,0:T(8,128)} %fusion.158, f32[1568,1536]{1,0:T(8,128)} %fusion.159, bf16[1568,768]{1,0:T(8,128)(2,1)} %param.19, bf16[1536,768]{1,0:T(8,128)(2,1)} %reshape.238), kind=kOutput, calls=%fused_computation.250 | convolution fusion | flops 3735502848 | bytes 38486016 | tf_op jit(solution)/shard_map/dot_general | solution.py:29
  410.6 6.7 fusion.160
  434.5 6.0 copy.78
  440.5 6.9 copy.79
  447.4 6.6 multiply_reduce_fusion.4
  454.5 10.1 fusion.86
  467.5 6.0 copy.87
  482.1 11.7 fusion.94
  503.6 175.3 %while.46 = (s32[]{:T(128)}, f32[384]{0:T(512)S(1)}, f32[384]{0:T(512)S(1)}, f32[28,56,384]{2,1,0:T(8,128)S(1)}, f32[28,56,384]{2,1,0:T(8,128)}, /*index=5*/f32[...) while((s32[]{:T(128)}, f32[384]{0:T(512)S(1)}, ...), condition=%wide.region_14.15_spmd.clone, body=%wide.region_9.0_spmd.clone.sunk | while | flops 6084100 | bytes 26491604 | solution.py:98
  680.4 9.2 fusion.113
  709.6 6.9 fusion.116
  729.1 9.8 fusion.163
  744.6 9.8 fusion.164
  760.3 9.8 fusion.165
  787.8 37.4 %all-reduce.87 = (f32[768]{0:T(1024)S(1)}, f32[768]{0:T(1024)S(1)}, f32[768]{0:T(1024)S(1)}, f32[384]{0:T(512)S(1)}, f32[384]{0:T(512)S(1)}) all-reduce(f32[768]{0:T(1024)S(1)} %get-tuple-element.454, f32[768]{0:T(1024)S(1)} %copy-done.36, f32[768]{0:T(1024)S(1)} %get-tuple-element.656, ...), channel_id=9, replica_groups=mesh['dp'=4,'fsdp'=8] {'dp','fsdp'}, use_global_device_ids=true, to_apply=%region_24.25.clone | all-reduce | flops 3072 | bytes 24576
  828.1 6.2 fusion.100
  834.4 8.3 add_convert_fusion
  842.7 51.0 %reduce-scatter.10.cloned.1.call-done = f32[144,128]{1,0:T(8,128)} async-done(((f32[4608,128]{1,0:T(8,128)}), f32[144,128]{1,0:T(8,128)}) %reduce-scatter.10.cloned.1.call-update) | async-done | bytes 73744 | tf_op jit(solution)/shard_map/reduce_scatter | solution.py:228
  893.7 104.8 %reduce-scatter.14.cloned.1.call-done = f32[144,128]{1,0:T(8,128)} async-done(((f32[4608,128]{1,0:T(8,128)}), f32[144,128]{1,0:T(8,128)}) %reduce-scatter.14.cloned.1.call-update) | async-done | bytes 73744 | tf_op jit(solution)/shard_map/reduce_scatter | solution.py:231
  998.4 103.8 %reduce-scatter.12.cloned.1.call-done = f32[144,128]{1,0:T(8,128)} async-done(((f32[4608,128]{1,0:T(8,128)}), f32[144,128]{1,0:T(8,128)}) %reduce-scatter.12.cloned.1.call-update) | async-done | bytes 73744 | tf_op jit(solution)/shard_map/reduce_scatter | solution.py:230
  1102.2 113.0 %reduce-scatter.16.cloned.1.call-done = f32[288,128]{1,0:T(8,128)} async-done(((f32[9216,128]{1,0:T(8,128)}), f32[288,128]{1,0:T(8,128)}) %reduce-scatter.16.cloned.1.call-update) | async-done | bytes 147472 | tf_op jit(solution)/shard_map/reduce_scatter | solution.py:232
  1215.2 112.0 %reduce-scatter.18.cloned.1.call-done = f32[288,128]{1,0:T(8,128)} async-done(((f32[9216,128]{1,0:T(8,128)}), f32[288,128]{1,0:T(8,128)}) %reduce-scatter.18.cloned.1.call-update) | async-done | bytes 147472 | tf_op jit(solution)/shard_map/reduce_scatter | solution.py:233
  1327.2 113.0 %reduce-scatter.20.cloned.1.call-done = f32[288,128]{1,0:T(8,128)} async-done(((f32[9216,128]{1,0:T(8,128)}), f32[288,128]{1,0:T(8,128)}) %reduce-scatter.20.cloned.1.call-update) | async-done | bytes 147472 | tf_op jit(solution)/shard_map/reduce_scatter | solution.py:234
  (2480 shorter events, 508.4 us)
Async XLA Ops:
  7.2 53.3 %copy-start.29 = (bf16[72,128]{1,0:T(8,128)(2,1)S(1)}, bf16[72,128]{1,0:T(8,128)(2,1)}, u32[]{:S(2)}) copy-start(bf16[72,128]{1,0:T(8,128)(2,1)} %param.21) | copy-start | bytes 55300
  7.2 100.8 %all-gather.7.cloned.1.call-start = ((), (), s32[]{:S(2)}) async-start(), calls=%async_computation.7 | async-start | bytes 1216512 | tf_op jit(solution)/shard_map/all_gather | solution.py:135
  7.9 334.4 %all-gather.9.cloned.1.call-start = ((), (), s32[]{:S(2)}) async-start(), calls=%async_computation.8 | async-start | bytes 1216512 | tf_op jit(solution)/shard_map/all_gather | solution.py:137
  8.7 337.1 %all-gather.11.cloned.1.call-start = ((), (), s32[]{:S(2)}) async-start(), calls=%async_computation.9 | async-start | bytes 1216512 | tf_op jit(solution)/shard_map/all_gather | solution.py:138
  9.4 353.1 %all-gather.13.cloned.1.call-start = ((), (), s32[]{:S(2)}) async-start(), calls=%async_computation.10 | async-start | bytes 2433024 | tf_op jit(solution)/shard_map/all_gather | solution.py:139
  10.0 358.5 %all-gather.15.cloned.1.call-start = ((), (), s32[]{:S(2)}) async-start(), calls=%async_computation.11 | async-start | bytes 2433024 | tf_op jit(solution)/shard_map/all_gather | solution.py:140
  10.6 377.7 %all-gather.17.cloned.1.call-start = ((), (), s32[]{:S(2)}) async-start(), calls=%async_computation.12 | async-start | bytes 2433024 | tf_op jit(solution)/shard_map/all_gather | solution.py:141
  11.1 831.5 %reduce-scatter.22.cloned.1.call-start = ((), (), s32[]{:S(2)}) async-start(), calls=%async_computation.19 | async-start | bytes 1216512
  57.6 53.9 %copy-start.34 = (bf16[384]{0:T(512)(128)(2,1)}, bf16[384]{0:T(512)(128)(2,1)S(1)}, u32[]{:S(2)}) copy-start(bf16[384]{0:T(512)(128)(2,1)S(1)} %get-tuple-element.516) | copy-start | bytes 2308
  57.6 291.6 %copy-start.27 = (f32[768]{0:T(1024)}, f32[768]{0:T(1024)S(1)}, u32[]{:S(2)}) copy-start(f32[768]{0:T(1024)S(1)} %convert_element_type.55) | copy-start | bytes 9220
  59.8 51.7 %copy-start.1 = (bf16[1568,768]{1,0:T(8,128)(2,1)S(1)}, bf16[1568,768]{1,0:T(8,128)(2,1)}, u32[]{:S(2)}) copy-start(bf16[1568,768]{1,0:T(8,128)(2,1)} %param.18) | copy-start | bytes 7225348
  59.9 289.3 %copy-start.21 = (f32[1568]{0:T(1024)}, f32[1568]{0:T(1024)S(1)}, u32[]{:S(2)}) copy-start(f32[1568]{0:T(1024)S(1)} %fusion.124) | copy-start | bytes 18820
  59.9 57.1 %copy-start.30 = (f32[384]{0:T(512)}, f32[384]{0:T(512)S(1)}, u32[]{:S(2)}) copy-start(f32[384]{0:T(512)S(1)} %get-tuple-element.669) | copy-start | bytes 4612
  59.9 57.1 %copy-start.32 = (f32[384]{0:T(512)}, f32[384]{0:T(512)S(1)}, u32[]{:S(2)}) copy-start(f32[384]{0:T(512)S(1)} %get-tuple-element.670) | copy-start | bytes 4612
  107.9 9.2 copy-start.15
  349.2 8.1 copy-start.10
  362.4 19.7 %copy-start.13 = (bf16[1568,768]{1,0:T(8,128)(2,1)}, bf16[1568,768]{1,0:T(8,128)(2,1)S(1)}, u32[]{:S(2)}) copy-start(bf16[1568,768]{1,0:T(8,128)(2,1)S(1)} %multiply_convert_fusion.3) | copy-start | bytes 7225348
  388.3 29.0 %slice-start = ((s8[4816896]{0:T(1024)(128)(4,1)}), s8[622592]{0:T(1024)(128)(4,1)S(1)}, s32[]{:S(2)}) async-start(s8[4816896]{0:T(1024)(128)(4,1)} %bitcast.292), calls=%async_computation.20 | async-start | bytes 1245184
  393.7 23.6 %slice-start.1 = ((s8[4816896]{0:T(1024)(128)(4,1)}), s8[4194304]{0:T(1024)(128)(4,1)S(1)}, s32[]{:S(2)}) async-start(s8[4816896]{0:T(1024)(128)(4,1)} %bitcast.292), calls=%async_computation.21 | async-start | bytes 8388608
  425.9 8.6 copy-start
  503.6 176.8 %copy-start.31 = (f32[384]{0:T(512)S(1)}, f32[384]{0:T(512)}, u32[]{:S(2)}) copy-start(f32[384]{0:T(512)} %copy-done.30) | copy-start | bytes 4612
  503.6 176.8 %copy-start.33 = (f32[384]{0:T(512)S(1)}, f32[384]{0:T(512)}, u32[]{:S(2)}) copy-start(f32[384]{0:T(512)} %copy-done.32) | copy-start | bytes 4612
  680.4 10.2 copy-start.3
  680.4 10.2 copy-start.22
  680.4 10.2 copy-start.28
  696.0 197.7 %reduce-scatter.10.cloned.1.call-start = ((), (), s32[]{:S(2)}) async-start(), calls=%async_computation.13 | async-start | bytes 2433024 | tf_op jit(solution)/shard_map/reduce_scatter | solution.py:228
  709.6 288.9 %reduce-scatter.14.cloned.1.call-start = ((), (), s32[]{:S(2)}) async-start(), calls=%async_computation.15 | async-start | bytes 2433024 | tf_op jit(solution)/shard_map/reduce_scatter | solution.py:231
  719.8 382.4 %reduce-scatter.12.cloned.1.call-start = ((), (), s32[]{:S(2)}) async-start(), calls=%async_computation.14 | async-start | bytes 2433024 | tf_op jit(solution)/shard_map/reduce_scatter | solution.py:230
  728.8 486.4 %reduce-scatter.16.cloned.1.call-start = ((), (), s32[]{:S(2)}) async-start(), calls=%async_computation.16 | async-start | bytes 4866048 | tf_op jit(solution)/shard_map/reduce_scatter | solution.py:232
  744.5 582.7 %reduce-scatter.18.cloned.1.call-start = ((), (), s32[]{:S(2)}) async-start(), calls=%async_computation.17 | async-start | bytes 4866048 | tf_op jit(solution)/shard_map/reduce_scatter | solution.py:233
  760.0 680.2 %reduce-scatter.20.cloned.1.call-start = ((), (), s32[]{:S(2)}) async-start(), calls=%async_computation.18 | async-start | bytes 4866048 | tf_op jit(solution)/shard_map/reduce_scatter | solution.py:234
  783.0 45.1 %copy-start.24 = (f32[1568]{0:T(1024)S(1)}, f32[1568]{0:T(1024)}, u32[]{:S(2)}) copy-start(f32[1568]{0:T(1024)} %copy-done.23) | copy-start | bytes 18820
  (26 other events, 101.0 us)
Sparse Core Ops, SparseCore 0:
  11.0 56.9 all-gather.6
  71.0 53.3 all-gather.8
  127.5 53.1 all-gather.10
  183.6 56.2 all-gather.12
  242.8 56.3 all-gather.14
  302.0 56.3 all-gather.16
  696.1 93.4 reduce-scatter.21
  795.5 98.1 reduce-scatter.9
  900.4 98.0 reduce-scatter.13
  1004.1 98.0 reduce-scatter.11
  1109.2 105.9 reduce-scatter.15
  1221.1 106.0 reduce-scatter.17
  1334.1 106.0 reduce-scatter.19
where the time goes:
time: 1460 us; the launch traced here: 1450 us
  waiting for transfers between devices  601 us (41%)
  local copies, waits for them, and re-layouts  296 us (20%)
  other arithmetic  261 us (18%)
  matrix products  139 us (10%)
  blocking collectives  125 us (9%)
  between operations  14.9 us (1%)
    reduce_scatter x1, waiting for transfers between devices, local(): lax.psum_scatter(all_terms[6], ('dp', 'fsdp'), scatter_dimension=0, tiled...  113 us
    reduce_scatter x1, waiting for transfers between devices, local(): lax.psum_scatter(all_terms[4], ('dp', 'fsdp'), scatter_dimension=0, tiled...  113 us
    reduce_scatter x1, waiting for transfers between devices, local(): lax.psum_scatter(all_terms[5], ('dp', 'fsdp'), scatter_dimension=0, tiled...  112 us
    reduce_scatter x1, waiting for transfers between devices, local(): lax.psum_scatter(all_terms[3], ('dp', 'fsdp'), scatter_dimension=0, tiled...  105 us
    reduce_scatter x1, waiting for transfers between devices, local(): lax.psum_scatter(all_terms[2], ('dp', 'fsdp'), scatter_dimension=0, tiled...  104 us
    squeeze x84, local copies, waits for them, and re-layouts, mixer_core(): lax.scan(jax.checkpoint(advance), initial, pieces)  79.5 us
    unnamed x2, blocking collectives  79.5 us
    add x252, other arithmetic, combine(): later_term[0] * earlier[3] + later_term[1] * earlier[2] + later_term[3]  69.3 us
  transfers between devices with their start and end apart: 13, of which 6 were waited for; matrix products, arithmetic and copies ran while one was open for 27% of the time, Pallas kernels for 0%

commit v1 on v0

--- a/solution.py
+++ b/solution.py
@@ -1,34 +1,878 @@
+import functools
+
 import jax
 import jax.numpy as jnp
 from jax import lax
+from jax.experimental import pallas as pl
+from jax.experimental.pallas import tpu as pltpu
 from jax.sharding import PartitionSpec as P
 
 D = 768
 C = 384
 FF = 1536
-SPAN = 56
 GROUPS = 8
-
+NB = D // 128
+CB = C // 128
 
 lower_bound = 0.25
 norm_eps = 1e-06
 group_eps = 1e-05
 
+F32 = jnp.float32
+BF16 = jnp.bfloat16
+MESH = pl.DeviceIdType.MESH
+MIB = 2**20
+
+DRIVE = (0, 24, 6)
+OUTGATE = (144, 24, 6)
+FORGET = (288, 24, 3)
+VECTORS = 360
+MIXOUT = (368, 24, 6)
+GATE = (512, 24, 12)
+UP = (800, 24, 12)
+DOWN = (1088, 48, 6)
+ROWS = 1376
+VECTOR_PARTS = ((0, 24), (24, 24), (48, 24), (72, 12), (84, 12))
+WDFG = 2 * D + C
+
+TILE = 224
+SEGMENTS = 16
+
+
+def sigmoid(t):
+    return 0.5 * jnp.tanh(0.5 * t) + 0.5
+
 
 def product(left, right):
-    return jnp.dot(left, right, preferred_element_type=jnp.float32)
+    return jnp.dot(left, right, preferred_element_type=F32)
+
+
+def back_product(left, right):
+    return lax.dot_general(left, right, (((1,), (1,)), ((), ())), preferred_element_type=F32)
 
 
 def outer_sum(left, right):
-    return lax.dot_general(
-        left, right, (((0,), (0,)), ((), ())), preferred_element_type=jnp.float32
-    )
-
-
-def back_product(left, right):
-    return lax.dot_general(
-        left, right, (((1,), (1,)), ((), ())), preferred_element_type=jnp.float32
-    )
+    return lax.dot_general(left, right, (((0,), (0,)), ((), ())), preferred_element_type=F32)
+
+
+def coords():
+    dp = lax.axis_index("dp")
+    fsdp = lax.axis_index("fsdp")
+    return dp // 2, dp % 2, fsdp // 2, fsdp % 2
+
+
+def device(y, x, z, core):
+    return (y * 2 + x, z * 2 + core)
+
+
+class Places:
+    def __init__(self):
+        y, x, z, c = coords()
+        self.z, self.core = z, c
+        fy = jnp.where(c == 0, 1 - y, y)
+        fx = jnp.where(c == 0, x, 1 - x)
+        sy = jnp.where(c == 0, y, 1 - y)
+        sx = jnp.where(c == 0, 1 - x, x)
+        self.first = device(fy, fx, z, c)
+        self.second = device(sy, sx, z, c)
+        self.sibling = device(y, x, z, 1 - c)
+        self.pair = device(y, x, z ^ 1, c)
+        self.along = [device(y, x, (z + d) % 4, c) for d in (1, 2, 3)]
+        self.col = (y * 2 + x) * 4
+        self.fcol = (fy * 2 + fx) * 4
+        self.scol = (sy * 2 + sx) * 4
+        self.dcol = ((1 - y) * 2 + (1 - x)) * 4
+        self.half = (z % 2) * 2
+        self.chip = self.col + z
+
+    def barrier(self):
+        bar = pltpu.get_barrier_semaphore()
+        for partner in [self.first, self.second, self.sibling] + self.along:
+            pl.semaphore_signal(bar, inc=1, device_id=partner, device_id_type=MESH)
+        pl.semaphore_wait(bar, 6)
+
+
+class Gather:
+    def __init__(self, places, raw, cuts, sems):
+        self.at, self.raw, self.cuts = places, raw, cuts
+        self.zs, self.zr, self.fs, self.fr, self.ss, self.sr, self.ps, self.pr, self.cs, self.cr = sems
+        self.ops = {}
+
+    @staticmethod
+    def semaphores(k):
+        dma = pltpu.SemaphoreType.DMA
+        return [dma((k, 3)), dma((k, 3)), dma((k,)), dma((k,)), dma((k, 2)), dma((k, 2)), dma((k,)), dma((k,)), dma((k, 5)), dma((k, 5))]
+
+    def send(self, key, first, count, k, send_sem, recv_sem, target):
+        low, high = self.cuts[k]
+        ref = self.raw.at[self.at.core, pl.ds(first, count), low:high]
+        copy = pltpu.make_async_remote_copy(
+            src_ref=ref, dst_ref=ref, send_sem=send_sem, recv_sem=recv_sem, device_id=target, device_id_type=MESH
+        )
+        copy.start()
+        self.ops[(key, k)] = copy
+
+    def along(self, k):
+        for d in range(3):
+            self.send(f"z{d}", self.at.chip, 1, k, self.zs.at[k, d], self.zr.at[k, d], self.at.along[d])
+
+    def column(self, k):
+        for d in range(3):
+            self.ops[(f"z{d}", k)].wait_recv()
+        at = self.at
+        self.send("f", at.col, 4, k, self.fs.at[k], self.fr.at[k], at.first)
+        self.send("s", at.col, 4, k, self.ss.at[k, 0], self.sr.at[k, 0], at.second)
+        self.send("c0", at.col, 4, k, self.cs.at[k, 0], self.cr.at[k, 0], at.sibling)
+
+    def plane(self, k):
+        at = self.at
+        self.ops[("f", k)].wait_recv()
+        self.send("s2", at.fcol + at.half, 2, k, self.ss.at[k, 1], self.sr.at[k, 1], at.second)
+        self.send("c1", at.fcol, 4, k, self.cs.at[k, 1], self.cr.at[k, 1], at.sibling)
+        self.ops[("s", k)].wait_recv()
+        self.send("c2", at.scol, 4, k, self.cs.at[k, 2], self.cr.at[k, 2], at.sibling)
+
+    def diagonal(self, k):
+        at = self.at
+        self.ops[("s2", k)].wait_recv()
+        self.send("p", at.dcol + at.half, 2, k, self.ps.at[k], self.pr.at[k], at.pair)
+        self.send("c3", at.dcol + at.half, 2, k, self.cs.at[k, 3], self.cr.at[k, 3], at.sibling)
+
+    def rest(self, k):
+        at = self.at
+        self.ops[("p", k)].wait_recv()
+        self.send("c4", at.dcol + 2 - at.half, 2, k, self.cs.at[k, 4], self.cr.at[k, 4], at.sibling)
+
+    def whole(self, k):
+        for i in range(5):
+            self.ops[(f"c{i}", k)].wait_recv()
+
+    def finish(self):
+        for copy in self.ops.values():
+            copy.wait_send()
+
+
+GATHER_SIZES = (144, 144, 80, 144, 144, 144, 144, 144, 144, 144)
+
+
+def cuts_of(sizes):
+    cuts, start = [], 0
+    for size in sizes:
+        cuts.append((start, start + size))
+        start += size
+    return cuts
+
+
+def pack(weight_ref, stage, blocks):
+    rows = weight_ref.shape[0]
+    stage[0:rows] = weight_ref[...].astype(F32)
+    each = rows // blocks
+    return jnp.concatenate([stage[pl.ds(j, each, stride=blocks)] for j in range(blocks)], axis=0)
+
+
+def assemble(raw, part, target, column):
+    first, rows, blocks = part
+    total = -(-rows * blocks // 16) * 16
+
+    def one(chip, _):
+        pair = [raw[core, chip, first : first + total].astype(F32) for core in (0, 1)]
+        for j in range(blocks):
+            block = jnp.concatenate([member[j * rows : (j + 1) * rows] for member in pair], axis=0)
+            target[pl.ds(pl.multiple_of(chip * (2 * rows), 16), 2 * rows), column + j * 128 : column + (j + 1) * 128] = (
+                block.astype(BF16)
+            )
+        return 0
+
+    lax.fori_loop(0, 16, one, 0)
+
+
+def spread(lane, width, total, by_row):
+    col = lax.broadcasted_iota(jnp.int32, (128, total), 1).astype(F32)
+    row = lax.broadcasted_iota(jnp.int32, (128, total), 0).astype(F32)
+    within = col - width * jnp.floor((col + 0.5) * (1.0 / width))
+    return jnp.where(row == within + lane, 1.0, 0.0).astype(BF16)
+
+
+def own_columns(width, total):
+    col = lax.broadcasted_iota(jnp.int32, (32, total), 1)
+    low = lax.broadcasted_iota(jnp.int32, (32, total), 0) * width
+    return jnp.logical_and(col >= low, col < low + width)
+
+
+def vector_of(rows, lane, width):
+    total = 32 * width
+    placed = product(rows, spread(lane, width, total, True))
+    return jnp.sum(jnp.where(own_columns(width, total), placed, 0.0), axis=0, keepdims=True)
+
+
+def col(c):
+    return slice(c * 128, (c + 1) * 128)
+
+
+def scan_forward(length, lam, src, out, cos, sin, carry):
+    steps = length // SEGMENTS
+    zero = jnp.zeros((SEGMENTS, 128), F32)
+
+    def rows(j):
+        return pl.ds(j, SEGMENTS, stride=steps)
+
+    def first(j, kept):
+        prod, re, im = kept
+        new_p, new_re, new_im = [], [], []
+        for c in range(CB):
+            gate = lam[c, rows(j)]
+            a, b = gate * cos[:, col(c)], gate * sin[:, col(c)]
+            new_p.append(prod[c] * gate)
+            new_re.append(a * re[c] - b * im[c] + src[c, rows(j)])
+            new_im.append(a * im[c] + b * re[c] + src[CB + c, rows(j)])
+        return tuple(new_p), tuple(new_re), tuple(new_im)
+
+    ones = (jnp.ones((SEGMENTS, 128), F32),) * CB
+    prod, re, im = lax.fori_loop(0, steps, first, (ones, (zero,) * CB, (zero,) * CB))
+    turn_re, turn_im = turned(cos, sin, steps)
+    for c in range(CB):
+        p_re, p_im = prod[c] * turn_re[:, col(c)], prod[c] * turn_im[:, col(c)]
+        at_re = at_im = jnp.zeros((1, 128), F32)
+        for k in range(SEGMENTS):
+            carry[c, k : k + 1] = at_re
+            carry[CB + c, k : k + 1] = at_im
+            row = slice(k, k + 1)
+            at_re, at_im = (
+                p_re[row] * at_re - p_im[row] * at_im + re[c][row],
+                p_re[row] * at_im + p_im[row] * at_re + im[c][row],
+            )
+
+    def second(j, kept):
+        re, im = kept
+        new_re, new_im = [], []
+        for c in range(CB):
+            gate = lam[c, rows(j)]
+            a, b = gate * cos[:, col(c)], gate * sin[:, col(c)]
+            new_re.append(a * re[c] - b * im[c] + src[c, rows(j)])
+            new_im.append(a * im[c] + b * re[c] + src[CB + c, rows(j)])
+            out[c, rows(j)] = new_re[c]
+            out[CB + c, rows(j)] = new_im[c]
+        return tuple(new_re), tuple(new_im)
+
+    start = tuple(carry[c] for c in range(CB)), tuple(carry[CB + c] for c in range(CB))
+    lax.fori_loop(0, steps, second, start)
+
+
+def turned(cos, sin, power):
+    re, im = jnp.ones_like(cos), jnp.zeros_like(sin)
+    base_re, base_im = cos, sin
+    while power:
+        if power % 2:
+            re, im = re * base_re - im * base_im, re * base_im + im * base_re
+        power //= 2
+        if power:
+            base_re, base_im = base_re * base_re - base_im * base_im, 2.0 * base_re * base_im
+    return re, im
+
+
+def opening_kernel(
+    length, cuts,
+    hidden, drive, forget, outgate, mixout, gate, up, down, vectors,
+    n1_out, pd_out, pg_out, lam_out, s_out, wdfg_out, wo_out, wau_out, wb_out, vec_out,
+    raw, stage, wdfg, wo, wau, wb, vec_rows, vec, n1, pd_low, pg_low, lam, src, states, carry,
+    out_sems, *sems,
+):
+    at = Places()
+    gather = Gather(at, raw, cuts, sems)
+    own = raw.at[at.core, at.chip]
+    for ref, part in ((drive, DRIVE), (outgate, OUTGATE), (mixout, MIXOUT), (gate, GATE), (up, UP), (down, DOWN)):
+        own[part[0] : part[0] + ref.shape[0]] = pack(ref, stage, part[2]).astype(BF16)
+    own[FORGET[0] : FORGET[0] + 80] = jnp.concatenate([pack(forget, stage, 3), vectors[...].astype(F32)], axis=0).astype(BF16)
+    at.barrier()
+
+    copies = []
+
+    def give(index, source, target):
+        copy = pltpu.make_async_copy(source, target, out_sems.at[index])
+        copy.start()
+        copies.append(copy)
+
+    def compute_first():
+        assemble(raw, DRIVE, wdfg, 0)
+        assemble(raw, FORGET, wdfg, D)
+        assemble(raw, OUTGATE, wdfg, D + C)
+        for chip in range(16):
+            for core in range(2):
+                block = raw[core, chip, FORGET[0] + 64 : FORGET[0] + 80].astype(F32)
+                vec_rows[2 * chip + core : 2 * chip + core + 1] = block[8:9]
+        rows = vec_rows[...].astype(BF16)
+        for index, (lane, width) in enumerate(VECTOR_PARTS):
+            vec[index : index + 1, 0 : 32 * width] = vector_of(rows, lane, width)
+        phase = vec[4:5, 0:C]
+        vec[5:6, 0:C] = jnp.cos(phase)
+        vec[6:7, 0:C] = jnp.sin(phase)
+        gain = vec[0:1]
+        bias = vec[3:4, 0:C]
+
+        def tile(t, _):
+            at_rows = pl.ds(pl.multiple_of(t * TILE, TILE), TILE)
+            x = hidden[at_rows].astype(F32)
+            normed = (x * lax.rsqrt(jnp.mean(x * x, axis=1, keepdims=True) + norm_eps) * gain).astype(BF16)
+            n1[at_rows] = normed
+            pre = product(normed, wdfg[...])
+            pd, pf, pg = pre[:, :D], pre[:, D : D + C], pre[:, D + C :]
+            pd_low[at_rows] = pd.astype(BF16)
+            pg_low[at_rows] = pg.astype(BF16)
+            keep = lower_bound + (1.0 - lower_bound) * sigmoid(pf + bias)
+            driven = pd * sigmoid(pd)
+            inflow = 1.0 - keep
+            for c in range(CB):
+                lam[c, at_rows] = keep[:, col(c)]
+                src[c, at_rows] = inflow[:, col(c)] * driven[:, col(c)]
+                src[CB + c, at_rows] = inflow[:, col(c)] * driven[:, col(CB + c)]
+            return 0
+
+        lax.fori_loop(0, length // TILE, tile, 0)
+        give(0, n1, n1_out)
+        give(1, pd_low, pd_out)
+        give(2, pg_low, pg_out)
+        give(3, lam, lam_out)
+        give(4, wdfg, wdfg_out)
+        give(5, vec, vec_out)
+
+    def compute_scan():
+        scan_forward(length, lam, src, states, vec[5:6, 0:C], vec[6:7, 0:C], carry)
+        give(6, states, s_out)
+
+    todo = {2: [compute_first, compute_scan], 3: [lambda: assemble(raw, MIXOUT, wo, 0), lambda: give(7, wo, wo_out)]}
+    todo[5] = [lambda: assemble(raw, GATE, wau, 0)]
+    todo[7] = [lambda: assemble(raw, UP, wau, FF), lambda: give(8, wau, wau_out)]
+    todo[9] = [lambda: assemble(raw, DOWN, wb, 0), lambda: give(9, wb, wb_out)]
+    count = len(cuts)
+    ahead = 2
+    for k in range(ahead):
+        gather.along(k)
+    for t in range(count + 5):
+        if t < count:
+            gather.column(t)
+            if t + ahead < count:
+                gather.along(t + ahead)
+        if 0 <= t - 1 < count:
+            gather.plane(t - 1)
+        if 0 <= t - 3 < count:
+            gather.diagonal(t - 3)
+        if 0 <= t - 4 < count:
+            gather.rest(t - 4)
+        if 0 <= t - 5 < count:
+            gather.whole(t - 5)
+            for work in todo.get(t - 5, ()):
+                work()
+    gather.finish()
+    for copy in copies:
+        copy.wait()
+
+
+def opening(hidden, weights, vectors):
+    length = hidden.shape[0]
+    cuts = cuts_of(GATHER_SIZES)
+    vmem = pl.BlockSpec(memory_space=pltpu.VMEM)
+    hbm = pl.BlockSpec(memory_space=pl.ANY)
+    shapes = [
+        ((length, D), BF16), ((length, D), BF16), ((length, D), BF16), ((CB, length, 128), F32), ((NB, length, 128), F32),
+        ((D, WDFG), BF16), ((D, D), BF16), ((D, 2 * FF), BF16), ((FF, D), BF16), ((8, D), F32),
+    ]
+    return pl.pallas_call(
+        functools.partial(opening_kernel, length, cuts),
+        out_shape=[jax.ShapeDtypeStruct(*s) for s in shapes],
+        in_specs=[vmem] * 9,
+        out_specs=[hbm] * len(shapes),
+        scratch_shapes=[
+            pltpu.VMEM((2, 16, ROWS, 128), BF16), pltpu.VMEM((288, 128), F32),
+            pltpu.VMEM((D, WDFG), BF16), pltpu.VMEM((D, D), BF16), pltpu.VMEM((D, 2 * FF), BF16), pltpu.VMEM((FF, D), BF16),
+            pltpu.VMEM((32, 128), F32), pltpu.VMEM((8, D), F32),
+            pltpu.VMEM((length, D), BF16), pltpu.VMEM((length, D), BF16), pltpu.VMEM((length, D), BF16),
+            pltpu.VMEM((CB, length, 128), F32), pltpu.VMEM((NB, length, 128), F32), pltpu.VMEM((NB, length, 128), F32),
+            pltpu.VMEM((NB, SEGMENTS, 128), F32),
+            pltpu.SemaphoreType.DMA((10,)),
+        ] + Gather.semaphores(len(cuts)),
+        compiler_params=pltpu.CompilerParams(collective_id=0, has_side_effects=True, vmem_limit_bytes=60 * MIB),
+    )(hidden, *weights, vectors)
+
+
+MID = 224
+
+
+def group_sum(values, ones, exact):
+    high = values.astype(BF16)
+    total = product(high, ones)
+    if exact:
+        total += product((values - high.astype(F32)).astype(BF16), ones)
+    return total
+
+
+def group_spread(values, wide):
+    high = values.astype(BF16)
+    low = (values - high.astype(F32)).astype(BF16)
+    return product(jnp.concatenate([high, low], axis=1), wide)
+
+
+def group_matrices():
+    feature = lax.broadcasted_iota(jnp.int32, (D, 128), 0)
+    group = lax.broadcasted_iota(jnp.int32, (D, 128), 1) * (D // GROUPS)
+    ones = jnp.where(jnp.logical_and(feature >= group, feature < group + D // GROUPS), 1.0, 0.0)
+    feature = lax.broadcasted_iota(jnp.int32, (256, D), 1)
+    row = lax.broadcasted_iota(jnp.int32, (256, D), 0)
+    group = jnp.where(row >= 128, row - 128, row) * (D // GROUPS)
+    wide = jnp.where(jnp.logical_and(feature >= group, feature < group + D // GROUPS), 1.0, 0.0)
+    return ones.astype(BF16), wide.astype(BF16)
+
+
+def middle_kernel(
+    x_ref, g_ref, s_ref, pg_ref, wo, wau, wb, vec,
+    out_ref, n2_ref, mixed_ref, units_ref, dpau_ref, dm_ref, dmiddle_ref, ds_ref, dpg_ref, sums_ref,
+    ones_ref, wide_ref,
+):
+    @pl.when(pl.program_id(0) == 0)
+    def _():
+        ones_ref[...], wide_ref[...] = group_matrices()
+        sums_ref[...] = jnp.zeros_like(sums_ref)
+
+    ones, wide = ones_ref[...], wide_ref[...]
+    share = 1.0 / (D // GROUPS)
+    second_gain, group_gain = vec[1:2], vec[2:3]
+    x = x_ref[...].astype(F32)
+    g = g_ref[...]
+    y = jnp.concatenate([s_ref[c] for c in range(NB)], axis=1)
+    centered = y - group_spread(group_sum(y, ones, True) * share, wide)
+    spread_var = group_sum(centered * centered, ones, False) * share
+    rstd = group_spread(lax.rsqrt(spread_var + group_eps), wide)
+    normed = centered * rstd
+    sg = sigmoid(pg_ref[...].astype(F32))
+    gated = group_gain * sg
+    mixed = (normed * gated).astype(BF16)
+    mixed_ref[...] = mixed
+    middle = x + product(mixed, wo[...])
+    q = lax.rsqrt(jnp.mean(middle * middle, axis=1, keepdims=True) + norm_eps)
+    scaled = middle * q
+    n2 = (scaled * second_gain).astype(BF16)
+    n2_ref[...] = n2
+    pre = product(n2, wau[...])
+    pa, pu = pre[:, :FF], pre[:, FF:]
+    sa = sigmoid(pa)
+    silu = pa * sa
+    units = (silu * pu).astype(BF16)
+    units_ref[...] = units
+    out_ref[...] = (middle + product(units, wb[...])).astype(BF16)
+    dunits = back_product(g, wb[...])
+    dpa = (dunits * pu * (sa * (1.0 + pa * (1.0 - sa)))).astype(BF16)
+    dpu = (dunits * silu).astype(BF16)
+    dpau = jnp.concatenate([dpa, dpu], axis=1)
+    dpau_ref[...] = dpau
+    dn2 = back_product(dpau, wau[...])
+    along = dn2 * scaled
+    h_mean = jnp.mean(along * second_gain, axis=1, keepdims=True)
+    dmiddle = g.astype(F32) + q * (second_gain * dn2 - scaled * h_mean)
+    dmiddle_ref[...] = dmiddle
+    dm = dmiddle.astype(BF16)
+    dm_ref[...] = dm
+    dmixed = back_product(dm, wo[...])
+    dnormed = dmixed * gated
+    both = dmixed * normed * sg
+    dpg_ref[...] = (both * group_gain * (1.0 - sg)).astype(BF16)
+    mean_one = group_spread(group_sum(dnormed, ones, False) * share, wide)
+    mean_two = group_spread(group_sum(dnormed * normed, ones, False) * share, wide)
+    ds = rstd * (dnormed - mean_one - normed * mean_two)
+    for c in range(NB):
+        ds_ref[c] = ds[:, col(c)]
+    sums_ref[0:1] += jnp.sum(along, axis=0, keepdims=True)
+    sums_ref[1:2] += jnp.sum(both, axis=0, keepdims=True)
+
+
+def middle_part(hidden, cotangent, states, pg, wo, wau, wb, vec):
+    length = hidden.shape[0]
+    rows = lambda width: pl.BlockSpec((MID, width), lambda t: (t, 0))
+    cols = pl.BlockSpec((NB, MID, 128), lambda t: (0, t, 0))
+    whole = lambda a: pl.BlockSpec(a.shape, lambda t: (0, 0), pipeline_mode=pl.Buffered(1))
+    outs = [(D, BF16), (D, BF16), (D, BF16), (FF, BF16), (2 * FF, BF16), (D, BF16), (D, F32)]
+    return pl.pallas_call(
+        middle_kernel,
+        grid=(length // MID,),
+        out_shape=[jax.ShapeDtypeStruct((length, w), t) for w, t in outs]
+        + [jax.ShapeDtypeStruct((NB, length, 128), F32), jax.ShapeDtypeStruct((length, D), BF16), jax.ShapeDtypeStruct((8, D), F32)],
+        in_specs=[rows(D), rows(D), cols, rows(D), whole(wo), whole(wau), whole(wb), whole(vec)],
+        out_specs=[rows(w) for w, _ in outs] + [cols, rows(D), pl.BlockSpec((8, D), lambda t: (0, 0))],
+        scratch_shapes=[pltpu.VMEM((D, 128), BF16), pltpu.VMEM((256, D), BF16)],
+        compiler_params=pltpu.CompilerParams(vmem_limit_bytes=60 * MIB),
+    )(hidden, cotangent, states, pg, wo, wau, wb, vec)
+
+
+CHUNKS = ((1088, 144), (1232, 144), (512, 144), (656, 144), (800, 144), (944, 144), (368, 144), (0, 144), (144, 144), (288, 80))
+
+
+class Scatter:
+    def __init__(self, places, stage, recv1, recv2, recv3, recvz, outs, sems):
+        self.at, self.stage = places, stage
+        self.recv1, self.recv2, self.recv3, self.recvz, self.outs = recv1, recv2, recv3, recvz, outs
+        self.s1, self.r1, self.s2, self.r2, self.s3, self.r3, self.s4, self.r4 = sems
+        self.ops = {}
+
+    @staticmethod
+    def semaphores(k):
+        dma = pltpu.SemaphoreType.DMA
+        return [dma((k,)), dma((k,)), dma((k, 2)), dma((k, 2)), dma((k,)), dma((k,)), dma((k, 3)), dma((k, 3))]
+
+    def send(self, key, source, target, send_sem, recv_sem, partner):
+        copy = pltpu.make_async_remote_copy(
+            src_ref=source, dst_ref=target, send_sem=send_sem, recv_sem=recv_sem, device_id=partner, device_id_type=MESH
+        )
+        copy.start()
+        self.ops[key] = copy
+
+    def rows(self, k):
+        return slice(CHUNKS[k][0], CHUNKS[k][0] + CHUNKS[k][1])
+
+    def add(self, k, first, received, slot):
+        rows, core = self.rows(k), self.at.core
+
+        def one(i, _):
+            mine = self.stage[core, first + i, rows].astype(F32)
+            self.stage[core, first + i, rows] = (mine + received[slot + i, rows].astype(F32)).astype(BF16)
+            return 0
+
+        lax.fori_loop(0, 4, one, 0)
+
+    def cores(self, k):
+        rows = self.rows(k)
+        self.send(("1", k), self.stage.at[1 - self.at.core, :, rows], self.recv1.at[:, rows], self.s1.at[k], self.r1.at[k], self.at.sibling)
+
+    def second(self, k):
+        rows, at = self.rows(k), self.at
+        self.ops[("1", k)].wait_recv()
+        for i, first in enumerate((at.dcol, at.scol)):
+            self.add(k, first, self.recv1, first)
+            self.send(
+                (f"2{i}", k), self.stage.at[at.core, pl.ds(first, 4), rows], self.recv2.at[pl.ds(4 * i, 4), rows],
+                self.s2.at[k, i], self.r2.at[k, i], at.second,
+            )
+        self.add(k, at.fcol, self.recv1, at.fcol)
+        self.add(k, at.col, self.recv1, at.col)
+
+    def first(self, k):
+        rows, at = self.rows(k), self.at
+        self.ops[("20", k)].wait_recv()
+        self.add(k, at.fcol, self.recv2, 0)
+        self.send(("3", k), self.stage.at[at.core, pl.ds(at.fcol, 4), rows], self.recv3.at[:, rows], self.s3.at[k], self.r3.at[k], at.first)
+        self.ops[("21", k)].wait_recv()
+        self.add(k, at.col, self.recv2, 4)
+
+    def along(self, k):
+        rows, at = self.rows(k), self.at
+        self.ops[("3", k)].wait_recv()
+        self.add(k, at.col, self.recv3, 0)
+        for d in (1, 2, 3):
+            self.send(
+                (f"4{d}", k), self.stage.at[at.core, at.col + (at.z + d) % 4, rows], self.recvz.at[d - 1, rows],
+                self.s4.at[k, d - 1], self.r4.at[k, d - 1], at.along[d - 1],
+            )
+
+    def last(self, k):
+        rows, at = self.rows(k), self.at
+        total = self.stage[at.core, at.chip, rows].astype(F32)
+        for d in (1, 2, 3):
+            self.ops[(f"4{d}", k)].wait_recv()
+            total += self.recvz[d - 1, rows].astype(F32)
+        self.outs(k, total)
+
+    def finish(self):
+        for copy in self.ops.values():
+            copy.wait_send()
+
+
+def closing_kernel(
+    length,
+    units, g, n2, dpau, mixed, dm, n1, dpg, states, ds, lam, pd, hidden, dmiddle, wdfg, vec, sums,
+    hidden_grad, drive_out, forget_out, outgate_out, mixout_out, gate_out, up_out, down_out, vec_out,
+    left, right, left2, right2, s_buf, ds_buf, lam_buf, wdfg_buf, x_tile, dm_tile, hg_tile, carry, vec_rows, vec_sums,
+    stage, recv1, recv2, recv3, recvz, load_sems, tile_sems, *sems,
+):
+    at = Places()
+
+    def unpack(ref, total, rows, blocks, first_block):
+        for j in range(total.shape[0] // rows):
+            ref[pl.ds(first_block + j, rows, stride=blocks)] = total[j * rows : (j + 1) * rows]
+
+    def deliver(k, total):
+        if k < 2:
+            unpack(down_out, total, 48, 6, 3 * k)
+        elif k < 4:
+            unpack(gate_out, total, 24, 12, 6 * (k - 2))
+        elif k < 6:
+            unpack(up_out, total, 24, 12, 6 * (k - 4))
+        elif k < 9:
+            unpack((mixout_out, drive_out, outgate_out)[k - 6], total, 24, 6, 0)
+        else:
+            unpack(forget_out, total[:72], 24, 3, 0)
+            vec_out[...] = total[72:80]
+
+    scatter = Scatter(at, stage, recv1, recv2, recv3, recvz, deliver, sems)
+    loads = {}
+
+    def load(key, source, target):
+        copy = pltpu.make_async_copy(source, target, load_sems.at[len(loads)])
+        copy.start()
+        loads[key] = copy
+
+    def need(*keys):
+        for key in keys:
+            loads[key].wait()
+
+    load("units", units, left)
+    load("g", g, right)
+    load("n2", n2, left2)
+    load("dpau", dpau, right2)
+    load("s", states, s_buf.at[:, pl.ds(8, length)])
+    load("ds", ds, ds_buf)
+    load("lam", lam, lam_buf)
+    load("wdfg", wdfg, wdfg_buf)
+    at.barrier()
+
+    def weight_chunk(source, source_col, rows, per, other, other_col, blocks, start, tail=None):
+        for m in range(rows // 384):
+            value = outer_sum(
+                source[:, source_col + 384 * m : source_col + 384 * (m + 1)], other[:, other_col : other_col + 128 * blocks]
+            )
+            for i in range(384 // per):
+                index = m * (384 // per) + i
+                core, chip = index % 2, index // 2
+                parts = [value[i * per : (i + 1) * per, col(j)] for j in range(blocks)]
+                if tail is not None:
+                    row = tail[index : index + 1]
+                    parts += [row, jnp.zeros((7, 128), F32)]
+                block = jnp.concatenate(parts, axis=0)
+                stage[core, chip, start : start + block.shape[0]] = block.astype(BF16)
+
+    def down(i):
+        if i == 0:
+            need("units", "g")
+        weight_chunk(left, 0, FF, 48, right, 384 * i, 3, DOWN[0] + 144 * i)
+        if i == 1:
+            load("mixed", mixed, left.at[:, 0:D])
+            load("n1", n1, left.at[:, D : 2 * D])
+            load("dm", dm, right)
+
+    def gate_up(i):
+        if i == 0:
+            need("n2", "dpau")
+        weight_chunk(left2, 0, D, 24, right2, D * i, 6, GATE[0] + 144 * i)
+        if i == 3:
+            load("dpg", dpg, right2.at[:, D + C : WDFG])
+            load("pd", pd, left2)
+
+    def mixout():
+        need("mixed", "dm")
+        weight_chunk(left, 0, D, 24, right, 0, 6, MIXOUT[0])
+
+    def reverse():
+        need("s", "ds", "lam", "pd")
+        vec_sums[0:1] = jnp.zeros((1, D), F32)
+        scan_backward(length, lam_buf, s_buf, ds_buf, vec[5:6, 0:C], vec[6:7, 0:C], carry, vec_sums)
+
+        def tile(t, _):
+            rows = pl.ds(pl.multiple_of(t * TILE, TILE), TILE)
+            pre = left2[rows].astype(F32)
+            sig = sigmoid(pre)
+            driven = pre * sig
+            slope = sig * (1.0 + pre * (1.0 - sig))
+            for c in range(CB):
+                gate = lam_buf[c, rows]
+                inflow = 1.0 - gate
+                dgate = s_buf[c, pl.ds(pl.multiple_of(t * TILE + 8, 8), TILE)]
+                for half in (c, CB + c):
+                    grad = ds_buf[half, rows]
+                    dgate -= grad * driven[:, col(half)]
+                    right2[rows, col(half)] = (inflow * grad * slope[:, col(half)]).astype(BF16)
+                dpf = dgate * ((gate - lower_bound) * inflow * (1.0 / (1.0 - lower_bound)))
+                vec_sums[0:1, col(c)] += jnp.sum(dpf, axis=0, keepdims=True)
+                right2[rows, col(NB + c)] = dpf.astype(BF16)
+            return 0
+
+        lax.fori_loop(0, length // TILE, tile, 0)
+
+    def drive():
+        need("n1", "dpg")
+        weight_chunk(left, D, D, 24, right2, 0, 6, DRIVE[0])
+
+    def outgate():
+        weight_chunk(left, D, D, 24, right2, D + C, 6, OUTGATE[0])
+
+    def inputs():
+        need("wdfg")
+        vec_sums[2:3] = jnp.zeros((1, D), F32)
+        first_gain = vec[0:1]
+        count = length // TILE
+        back = {}
+
+        def fetch(t):
+            rows = slice(t * TILE, (t + 1) * TILE)
+            a = pltpu.make_async_copy(hidden.at[rows], x_tile.at[t % 2], tile_sems.at[0, t % 2])
+            b = pltpu.make_async_copy(dmiddle.at[rows], dm_tile.at[t % 2], tile_sems.at[1, t % 2])
+            a.start()
+            b.start()
+            back[t] = (a, b)
+
+        fetch(0)
+        outgoing = {}
+        for t in range(count):
+            if t + 1 < count:
+                fetch(t + 1)
+            for copy in back[t]:
+                copy.wait()
+            rows = slice(t * TILE, (t + 1) * TILE)
+            x = x_tile[t % 2].astype(F32)
+            dn1 = back_product(right2[rows, 0:WDFG], wdfg_buf[...])
+            p = lax.rsqrt(jnp.mean(x * x, axis=1, keepdims=True) + norm_eps)
+            scaled = x * p
+            terms = dn1 * scaled
+            vec_sums[2:3] += jnp.sum(terms, axis=0, keepdims=True)
+            if t >= 2:
+                outgoing[t - 2].wait()
+            mean = jnp.mean(terms * first_gain, axis=1, keepdims=True)
+            hg_tile[t % 2] = dm_tile[t % 2] + p * (first_gain * dn1 - scaled * mean)
+            copy = pltpu.make_async_copy(hg_tile.at[t % 2], hidden_grad.at[rows], tile_sems.at[2, t % 2])
+            copy.start()
+            outgoing[t] = copy
+        for t in (count - 2, count - 1):
+            outgoing[t].wait()
+
+    def forget():
+        rows = jnp.zeros((32, 128), F32)
+        sources = (vec_sums[2:3], sums[0:1], sums[1:2], vec_sums[0:1, 0:C], vec_sums[1:2, 0:C])
+        for (lane, width), source in zip(VECTOR_PARTS, sources):
+            total = 32 * width
+            mine = jnp.where(own_columns(width, total), jnp.broadcast_to(source, (32, total)), 0.0).astype(BF16)
+            rows += back_product(mine, spread(lane, width, total, True))
+        vec_rows[...] = rows
+        weight_chunk(left, D, D, 24, right2, D, 3, FORGET[0], vec_rows)
+
+    work = [
+        lambda: down(0), lambda: down(1), lambda: gate_up(0), lambda: gate_up(1), lambda: gate_up(2), lambda: gate_up(3), mixout,
+        lambda: (reverse(), drive()), outgate, lambda: (inputs(), forget()),
+    ]
+    count = len(work)
+    for t in range(count + 4):
+        if t < count:
+            work[t]()
+            scatter.cores(t)
+        if 0 <= t - 1 < count:
+            scatter.second(t - 1)
+        if 0 <= t - 2 < count:
+            scatter.first(t - 2)
+        if 0 <= t - 3 < count:
+            scatter.along(t - 3)
+        if 0 <= t - 4 < count:
+            scatter.last(t - 4)
+    scatter.finish()
+
+
+def scan_backward(length, lam, states, ds, cos, sin, carry, vec_sums):
+    steps = length // SEGMENTS
+    zero = jnp.zeros((SEGMENTS, 128), F32)
+
+    def rows(j):
+        return pl.ds(j, SEGMENTS, stride=steps)
+
+    def first(i, kept):
+        j = steps - 1 - i
+        prod, re, im = kept
+        new_p, new_re, new_im = [], [], []
+        for c in range(CB):
+            gate = lam[c, rows(j)]
+            g_re, g_im = ds[c, rows(j)] + re[c], ds[CB + c, rows(j)] + im[c]
+            new_p.append(prod[c] * gate)
+            new_re.append(gate * (cos[:, col(c)] * g_re + sin[:, col(c)] * g_im))
+            new_im.append(gate * (cos[:, col(c)] * g_im - sin[:, col(c)] * g_re))
+        return tuple(new_p), tuple(new_re), tuple(new_im)
+
+    ones = (jnp.ones((SEGMENTS, 128), F32),) * CB
+    prod, re, im = lax.fori_loop(0, steps, first, (ones, (zero,) * CB, (zero,) * CB))
+    turn_re, turn_im = turned(cos, -sin, steps)
+    for c in range(CB):
+        p_re, p_im = prod[c] * turn_re[:, col(c)], prod[c] * turn_im[:, col(c)]
+        at_re = at_im = jnp.zeros((1, 128), F32)
+        for k in reversed(range(SEGMENTS)):
+            carry[c, k : k + 1] = at_re
+            carry[CB + c, k : k + 1] = at_im
+            row = slice(k, k + 1)
+            at_re, at_im = (
+                p_re[row] * at_re - p_im[row] * at_im + re[c][row],
+                p_re[row] * at_im + p_im[row] * at_re + im[c][row],
+            )
+    for c in range(NB):
+        states[c, 0:8] = jnp.zeros((8, 128), F32)
+
+    def step(at_rows, before, kept):
+        re, im, phase = kept
+        new_re, new_im, new_phase = [], [], []
+        for c in range(CB):
+            gate = lam[c, at_rows]
+            g_re, g_im = ds[c, at_rows] + re[c], ds[CB + c, at_rows] + im[c]
+            w_re = cos[:, col(c)] * g_re + sin[:, col(c)] * g_im
+            w_im = cos[:, col(c)] * g_im - sin[:, col(c)] * g_re
+            new_re.append(gate * w_re)
+            new_im.append(gate * w_im)
+            s_re, s_im = before(c), before(CB + c)
+            new_phase.append(phase[c] + gate * (w_im * s_re - w_re * s_im))
+            ds[c, at_rows] = g_re
+            ds[CB + c, at_rows] = g_im
+            yield c, w_re * s_re + w_im * s_im
+        kept[:] = [tuple(new_re), tuple(new_im), tuple(new_phase)]
+
+    opening_rows = [states[c, pl.ds(7, SEGMENTS, stride=steps)] for c in range(NB)]
+
+    def second(i, kept):
+        j = steps - 1 - i
+        kept = list(kept)
+        for c, dgate in step(rows(j), lambda c: states[c, pl.ds(j + 7, SEGMENTS, stride=steps)], kept):
+            states[c, pl.ds(j + 8, SEGMENTS, stride=steps)] = dgate
+        return tuple(kept)
+
+    start = (tuple(carry[c] for c in range(CB)), tuple(carry[CB + c] for c in range(CB)), (zero,) * CB)
+    kept = list(lax.fori_loop(0, steps - 1, second, start))
+    for c, dgate in step(rows(0), lambda c: opening_rows[c], kept):
+        states[c, pl.ds(8, SEGMENTS, stride=steps)] = dgate
+    for c in range(CB):
+        vec_sums[1:2, col(c)] = jnp.sum(kept[2][c], axis=0, keepdims=True)
+
+
+def closing(length, shards, arrays, hidden, dmiddle, wdfg, vec, sums):
+    vmem = pl.BlockSpec(memory_space=pltpu.VMEM)
+    hbm = pl.BlockSpec(memory_space=pl.ANY)
+    shapes = [(length, D)] + [w.shape for w in shards] + [(8, 128)]
+    return pl.pallas_call(
+        functools.partial(closing_kernel, length),
+        out_shape=[jax.ShapeDtypeStruct(s, F32) for s in shapes],
+        in_specs=[hbm] * 15 + [vmem] * 2,
+        out_specs=[hbm] + [vmem] * 8,
+        scratch_shapes=[
+            pltpu.VMEM((length, FF), BF16), pltpu.VMEM((length, D), BF16), pltpu.VMEM((length, D), BF16), pltpu.VMEM((length, 2 * FF), BF16),
+            pltpu.VMEM((NB, length + 8, 128), F32), pltpu.VMEM((NB, length, 128), F32), pltpu.VMEM((CB, length, 128), F32),
+            pltpu.VMEM((D, WDFG), BF16), pltpu.VMEM((2, TILE, D), BF16), pltpu.VMEM((2, TILE, D), F32), pltpu.VMEM((2, TILE, D), F32),
+            pltpu.VMEM((NB, SEGMENTS, 128), F32), pltpu.VMEM((32, 128), F32), pltpu.VMEM((8, D), F32),
+            pltpu.VMEM((2, 16, ROWS, 128), BF16), pltpu.VMEM((16, ROWS, 128), BF16), pltpu.VMEM((8, ROWS, 128), BF16),
+            pltpu.VMEM((4, ROWS, 128), BF16), pltpu.VMEM((3, ROWS, 128), BF16),
+            pltpu.SemaphoreType.DMA((16,)), pltpu.SemaphoreType.DMA((3, 2)),
+        ] + Scatter.semaphores(len(CHUNKS)),
+        compiler_params=pltpu.CompilerParams(collective_id=1, has_side_effects=True, vmem_limit_bytes=62 * MIB),
+    )(*arrays, hidden, dmiddle, wdfg, vec, sums)
+
+
+def fast(hidden, cotangent, *params):
+    weights, parts = params[:7], params[7:]
+    vectors = jnp.zeros((8, 128), BF16).at[0, :96].set(jnp.concatenate(parts))
+    n1, pd, pg, lam, states, wdfg, wo, wau, wb, vec = opening(hidden, weights, vectors)
+    out, n2, mixed, units, dpau, dm, dmiddle, ds, dpg, sums = middle_part(hidden, cotangent, states, pg, wo, wau, wb, vec)
+    hidden_grad, *grads, row = closing(
+        hidden.shape[0], weights, (units, cotangent, n2, dpau, mixed, dm, n1, dpg, states, ds, lam, pd), hidden, dmiddle, wdfg, vec, sums
+    )
+    return (out, hidden_grad, *grads) + tuple(row[0, lane : lane + width] for lane, width in VECTOR_PARTS)
+
+
+SPAN = 56
 
 
 def rms_scale(values, gain_vec):
@@ -257,36 +1101,8 @@
 
 
 def solution(mesh):
-    in_specs = (
-        P(("dp", "fsdp"), None),
-        P(("dp", "fsdp"), None),
-        P(("dp", "fsdp"), None),
-        P(("dp", "fsdp"), None),
-        P(("dp", "fsdp"), None),
-        P(("dp", "fsdp"), None),
-        P(("dp", "fsdp"), None),
-        P(("dp", "fsdp"), None),
-        P(("dp", "fsdp"), None),
-        P(("dp", "fsdp")),
-        P(("dp", "fsdp")),
-        P(("dp", "fsdp")),
-        P(("dp", "fsdp")),
-        P(("dp", "fsdp")),
-    )
-    out_specs = (
-        P(("dp", "fsdp"), None),
-        P(("dp", "fsdp"), None),
-        P(("dp", "fsdp"), None),
-        P(("dp", "fsdp"), None),
-        P(("dp", "fsdp"), None),
-        P(("dp", "fsdp"), None),
-        P(("dp", "fsdp"), None),
-        P(("dp", "fsdp"), None),
-        P(("dp", "fsdp"), None),
-        P(("dp", "fsdp")),
-        P(("dp", "fsdp")),
-        P(("dp", "fsdp")),
-        P(("dp", "fsdp")),
-        P(("dp", "fsdp")),
-    )
-    return jax.shard_map(local, mesh=mesh, in_specs=in_specs, out_specs=out_specs, check_vma=False)
+    rows, flat = P(("dp", "fsdp"), None), P(("dp", "fsdp"))
+    step = fast if dict(mesh.shape) == {"dp": 4, "fsdp": 8} else local
+    return jax.shard_map(
+        step, mesh=mesh, in_specs=(rows,) * 9 + (flat,) * 5, out_specs=(rows,) * 9 + (flat,) * 5, check_vma=False
+    )

time: 1460 us -> 231 us (0.16)
  waiting for transfers between devices: 601 us -> 0 us
  local copies, waits for them, and re-layouts: 296 us -> 16.2 us
  other arithmetic: 261 us -> 0 us
  Pallas kernels: 0 us -> 214 us
  matrix products: 139 us -> 0 us
  blocking collectives: 125 us -> 0 us
    reduce_scatter x6 -> x0, waiting for transfers between devices: 598 us -> none  [the longest x1 113 us: local(): lax.psum_scatter(all_terms[6], ('dp', 'fsdp'), scatter_dimension=0, tiled...]
    pallas_call x0 -> x3, Pallas kernels: none -> 214 us  [the longest x1 87.6 us: closing(): pl.pallas_call(functools.partial(closing_kernel, length), out_shape=[jax....]
    dot_general x21 -> x0, matrix products: 139 us -> none  [the longest x7 48.9 us: outer_sum(): lax.dot_general(left, right, (((0,), (0,)), ((), ())), preferred_element_...]
    add x422 -> x0, other arithmetic: 85.5 us -> none  [the longest x252 69.3 us: combine(): later_term[0] * earlier[3] + later_term[1] * earlier[2] + later_term[3]]
    unnamed x2 -> x0, blocking collectives: 79.5 us -> none
    squeeze x84 -> x2, local copies, waits for them, and re-layouts: 79.5 us -> 2.73 us  [fast(): row[0, lane:lane + width]]
    reshape x15 -> x0, local copies, waits for them, and re-layouts: 65.3 us -> none  [the longest x7 29.2 us: unpack(): gathered[position].reshape(target)]
    dynamic_update_slice x84 -> x0, other arithmetic: 61 us -> none  [mixer_core(): lax.scan(jax.checkpoint(advance), initial, pieces)]
  transfers between devices with their start and end apart: 13 -> 0, of which waited for: 6 -> 0; matrix products, arithmetic and copies ran while one was open for 27% -> 0% of each run, Pallas kernels for 0% -> 0%
where the time goes in v1:
time: 231 us
  Pallas kernels  214 us (93%)
  local copies, waits for them, and re-layouts  16.2 us (7%)
    pallas_call x1, Pallas kernels, closing(): pl.pallas_call(functools.partial(closing_kernel, length), out_shape=[jax....  87.6 us
    pallas_call x1, Pallas kernels, opening(): pl.pallas_call(functools.partial(opening_kernel, length, cuts), out_shape...  72.2 us
    pallas_call x1, Pallas kernels, middle_part(): pl.pallas_call(middle_kernel, grid=(length // MID,), out_shape=[jax.Shape...  53.9 us
    unnamed x22, local copies, waits for them, and re-layouts  9.49 us

profile of v1, /device:TPU:0, one launch (start us, length us, event | category | flops | bytes accessed | tf_op | source)
XLA Modules:
  0.0 230.6 jit_solution(10971167026885469205)
XLA Ops:
  0.6 3.4 %concatenate.5 = bf16[96]{0:T(256)(128)(2,1)S(1)} concatenate(bf16[24]{0:T(256)(128)(2,1)} %param.25, bf16[24]{0:T(256)(128)(2,1)} %param.26, bf16[24]{0:T(256)(128)(2,1)} %param.27, bf16[12]{0:T(256)(128)(2,1)} %param.28, bf16[12]{0:T(256)(128)(2,1)} %param.29), dimensions={0} | concatenate | bytes 384 | tf_op jit(solution)/shard_map/concatenate | solution.py:866
  4.1 0.6 scatter.4.vectors
  4.7 72.2 %shard_map.245 = (bf16[1568,768]{1,0:T(8,128)(2,1)}, bf16[1568,768]{1,0:T(8,128)(2,1)}, bf16[1568,768]{1,0:T(8,128)(2,1)}, f32[3,1568,128]{2,1,0:T(8,128)}, f32[...) custom-call(bf16[1568,768]{1,0:T(8,128)(2,1)} %hidden.3, ...), custom_call_target="tpu_custom_call" | custom-call | tf_op jit(solution)/shard_map/pallas_call | solution.py:379
  76.8 53.9 %shard_map.246 = (bf16[1568,768]{1,0:T(8,128)(2,1)}, bf16[1568,768]{1,0:T(8,128)(2,1)}, bf16[1568,768]{1,0:T(8,128)(2,1)}, bf16[1568,1536]{1,0:T(8,128)(2,1)}, b...) custom-call(bf16[1568,768]{1,0:T(8,128)(2,1)} %hidden.3, ...), custom_call_target="tpu_custom_call" | custom-call | tf_op jit(solution)/shard_map/pallas_call | solution.py:492
  130.8 87.6 %shard_map.247 = (f32[1568,768]{1,0:T(8,128)}, f32[144,128]{1,0:T(8,128)}, f32[72,128]{1,0:T(8,128)}, f32[144,128]{1,0:T(8,128)}, f32[144,128]{1,0:T(8,128)}, /*...) custom-call(bf16[1568,1536]{1,0:T(8,128)(2,1)} %get-tuple-element.62.units, ...), custom_call_target="tpu_custom_call" | custom-call | tf_op jit(solution)/shard_map/pallas_call | solution.py:846
  218.3 1.3 slice_bitcast_fusion
  219.7 1.4 slice_bitcast_fusion.2
  221.0 0.0 copy-start.5
  221.0 0.0 copy-start.6
  221.0 0.0 copy-start.4
  221.1 0.0 copy-start.3
  221.1 0.0 copy-start.2
  221.1 0.0 copy-start.1
  221.1 0.0 copy-start
  221.1 5.0 %copy.36 = f32[1568,768]{1,0:T(8,128)} copy(f32[1568,768]{1,0:T(8,128)} %get-tuple-element.104) | data formatting | bytes 9633792
  226.1 0.0 copy-done.5
  226.1 0.6 copy.37
  226.7 0.0 copy-done.6
  226.7 0.6 copy.38
  227.3 0.0 copy-done.4
  227.3 0.6 copy.39
  227.9 0.0 copy-done.3
  227.9 0.6 copy.40
  228.6 0.0 copy-done.2
  228.6 0.7 copy.41
  229.2 0.0 copy-done.1
  229.2 0.7 copy.42
  229.9 0.0 copy-done
  229.9 0.7 copy.43
Async XLA Ops:
  221.0 5.0 %copy-start.5 = (f32[144,128]{1,0:T(8,128)S(1)}, f32[144,128]{1,0:T(8,128)}, u32[]{:S(2)}) copy-start(f32[144,128]{1,0:T(8,128)} %get-tuple-element.105) | copy-start | bytes 221188
  221.0 5.6 %copy-start.6 = (f32[72,128]{1,0:T(8,128)S(1)}, f32[72,128]{1,0:T(8,128)}, u32[]{:S(2)}) copy-start(f32[72,128]{1,0:T(8,128)} %get-tuple-element.106) | copy-start | bytes 110596
  221.0 6.3 %copy-start.4 = (f32[144,128]{1,0:T(8,128)S(1)}, f32[144,128]{1,0:T(8,128)}, u32[]{:S(2)}) copy-start(f32[144,128]{1,0:T(8,128)} %get-tuple-element.107) | copy-start | bytes 221188
  221.1 6.9 %copy-start.3 = (f32[144,128]{1,0:T(8,128)S(1)}, f32[144,128]{1,0:T(8,128)}, u32[]{:S(2)}) copy-start(f32[144,128]{1,0:T(8,128)} %get-tuple-element.108) | copy-start | bytes 221188
  221.1 7.5 %copy-start.2 = (f32[288,128]{1,0:T(8,128)S(1)}, f32[288,128]{1,0:T(8,128)}, u32[]{:S(2)}) copy-start(f32[288,128]{1,0:T(8,128)} %get-tuple-element.109) | copy-start | bytes 442372
  221.1 8.2 %copy-start.1 = (f32[288,128]{1,0:T(8,128)S(1)}, f32[288,128]{1,0:T(8,128)}, u32[]{:S(2)}) copy-start(f32[288,128]{1,0:T(8,128)} %get-tuple-element.110) | copy-start | bytes 442372
  221.1 8.8 %copy-start = (f32[288,128]{1,0:T(8,128)S(1)}, f32[288,128]{1,0:T(8,128)}, u32[]{:S(2)}) copy-start(f32[288,128]{1,0:T(8,128)} %get-tuple-element.111) | copy-start | bytes 442372
